TPU v7x, 512 devices: a whole 4x4x16 slice. The times are simulated.
512 devices in a mesh: seg: 64 (over z_lo, x, core), vec: 8 (over y, z_hi).
Axes of the slice: x: 4, y: 4, z: 16 (z_hi: 2, z_lo: 8; z = z_hi * 8 + z_lo), core: 2. Of those that a mesh axis runs over, the one named last changes fastest.
Arguments:
- line_vectors: float32 [256, 393216], P('vec', 'seg')
- mode_vectors: float32 [256, 16384], P('vec', 'seg'), may hold values from -6 to 6
- line_diagonal: float32 [393216], P('seg'), may hold values from 2 to 4
- line_links: float32 [393216], P('seg'), may hold values from 0.2 to 0.9
- stiffness: float32 [16384], P('seg'), may hold values from 0.5 to 6
- coupling_tiles: bfloat16 [2816, 128, 256], P('seg'), may hold values from -0.1875 to 0.1875
- attachments: int32 [2816, 1], P('seg'), may hold values from 0 to 63; in each aligned block of 44 rows (0 to 43, 44 to 87, ...) at most 2 rows name the same one
- block_counts: int32 [64, 2], P('seg'), may hold values from 1 to 24, 44 in all within a row
Outputs:
- filtered_line: float32 [256, 393216], P('vec', 'seg')
- filtered_modes: float32 [256, 16384], P('vec', 'seg')
- gram_matrix: float32 [256, 256], P('vec')
Inputs may be any that keep to these rules, and one draw needn't show every extreme that they name: `attachments`: among the 44 rows of one device no mode block is named more than 2 times; some mode blocks are named by none of them. `block_counts`: each row sums to 44; attachments of a device are listed by segment block in order.
All inputs are finite; a program needn't handle non-finite values.
Results may differ from a plain program's by a relative error of at most 0.0005.
The roundings to bfloat16 on the way count: a program that leaves them out, or rounds other values in their place, can miss the bound.
Values may be sent and summed in bfloat16 or wider, within the bound.
A program may use at most 64 MiB of HBM per device.

v0:
```python
import jax
import jax.numpy as jnp
from jax import lax
from jax.sharding import PartitionSpec as P

PANEL = 128
PANELS = 24


center_shift = 3.0
half_width = 2.5


def padded_2(array, sides, width):
    for axis, dim in sides:
        size, length = (lax.axis_size(axis), array.shape[dim])
        up = [(i, (i + 1) % size) for i in range(size - 1)]
        down = [(j, i) for i, j in up]
        last = lax.slice_in_dim(array, length - width, length, axis=dim)
        first = lax.slice_in_dim(array, 0, width, axis=dim)
        before = lax.ppermute(last, axis, up)
        after = lax.ppermute(first, axis, down)
        array = jnp.concatenate([before, array, after], axis=dim)
    return array


def layout(per_block, owners):
    attached = owners.shape[0]
    positions = jnp.arange(attached, dtype=jnp.int32)
    block_ends = jnp.cumsum(per_block)
    block_starts = block_ends - per_block
    block_of = jnp.sum((positions[:, None] >= block_ends[None, :]).astype(jnp.int32), 1)
    chosen = block_of[:, None] == jnp.arange(per_block.shape[0], dtype=jnp.int32)[None, :]
    first_slot = jnp.sum(jnp.where(chosen, block_starts[None, :], 0), 1)
    return block_of * PANELS + positions - first_slot


def body(
    line_vectors,
    mode_vectors,
    line_diagonal,
    line_links,
    stiffness,
    coupling_tiles,
    attachments,
    block_counts,
):
    segment_count = lax.axis_size("seg")
    attached = coupling_tiles.shape[0]
    capacity = max(2, (2 * attached + segment_count - 1) // segment_count)
    columns = line_vectors.shape[0]
    line_rows = line_vectors.shape[1]
    mode_width = mode_vectors.shape[1]
    owners = attachments[:, 0]
    panel_index = layout(block_counts[0], owners)
    positions = jnp.arange(attached, dtype=jnp.int32)
    earlier_same = (owners[:, None] == owners[None, :]) & (positions[None, :] < positions[:, None])
    slot_index = owners * capacity + jnp.sum(earlier_same.astype(jnp.int32), 1)

    def operate(line_part, mode_part):
        stacked = jnp.stack([line_part, line_links * line_part])
        padded = padded_2(stacked, (("seg", 2),), 1)
        acoustic = line_diagonal * line_part - line_links * padded[0, :, 2:] - padded[1, :, :-2]
        everyone = lax.all_gather(mode_part.astype(jnp.bfloat16), "seg", axis=1, tiled=True)
        picked = jnp.take(everyone.reshape(columns, segment_count, mode_width), owners, axis=1)
        products = jnp.einsum(
            "vtm,tpm->vtp", picked, coupling_tiles, preferred_element_type=jnp.float32
        )
        coupled = (
            jnp.zeros((columns, line_rows // PANEL, PANEL), jnp.float32)
            .at[:, panel_index, :]
            .add(products)
        )
        panel_rows = line_part.astype(jnp.bfloat16).reshape(columns, line_rows // PANEL, PANEL)
        panels = jnp.take(panel_rows, panel_index, axis=1)
        outgoing = jnp.einsum(
            "vtp,tpm->tvm", panels, coupling_tiles, preferred_element_type=jnp.float32
        ).astype(jnp.bfloat16)
        selector = (
            slot_index[None, :] == jnp.arange(segment_count * capacity, dtype=jnp.int32)[:, None]
        ).astype(jnp.bfloat16)
        buffered = jnp.einsum(
            "st,tvm->svm", selector, outgoing, preferred_element_type=jnp.float32
        ).astype(jnp.bfloat16)
        arrived = lax.all_to_all(buffered, "seg", split_axis=0, concat_axis=0, tiled=True)
        summed = jnp.sum(arrived.astype(jnp.float32), 0)
        return (acoustic + coupled.reshape(columns, line_rows), stiffness * mode_part + summed)

    image_line, image_mode = operate(line_vectors, mode_vectors)
    first_line = (image_line - center_shift * line_vectors) / half_width
    first_mode = (image_mode - center_shift * mode_vectors) / half_width
    image_line, image_mode = operate(first_line, first_mode)
    filtered_line = 2.0 * (image_line - center_shift * first_line) / half_width - line_vectors
    filtered_modes = 2.0 * (image_mode - center_shift * first_mode) / half_width - mode_vectors
    rounded_line = filtered_line.astype(jnp.bfloat16)
    rounded_mode = filtered_modes.astype(jnp.bfloat16)
    dims = (((1,), (1,)), ((), ()))
    products = lax.dot_general(
        rounded_line,
        lax.all_gather(rounded_line, "vec", axis=0, tiled=True),
        dims,
        preferred_element_type=jnp.float32,
    )
    products = products + lax.dot_general(
        rounded_mode,
        lax.all_gather(rounded_mode, "vec", axis=0, tiled=True),
        dims,
        preferred_element_type=jnp.float32,
    )
    summed_gram = lax.psum(products, "seg")
    gram_matrix = summed_gram / float((line_rows + mode_width) * segment_count)
    return (filtered_line, filtered_modes, gram_matrix)


def solution(mesh):
    in_specs = (
        P("vec", "seg"),
        P("vec", "seg"),
        P("seg"),
        P("seg"),
        P("seg"),
        P("seg", None, None),
        P("seg", None),
        P("seg", None),
    )
    out_specs = (P("vec", "seg"), P("vec", "seg"), P("vec", None))
    return jax.shard_map(body, mesh=mesh, in_specs=in_specs, out_specs=out_specs, check_vma=False)
```

profile of v0, /device:TPU:1, one launch (start us, length us, event | category | flops | bytes accessed | tf_op | source)
XLA Modules:
  0.0 1021.3 jit_solution(12499395836966780087)
XLA Ops:
  7.2 1.0 reduce-window.4
  8.2 0.7 fusion.44
  8.9 0.9 convert_reduce_fusion.2
  9.8 0.7 multiply_add_fusion
  10.6 2.4 convert_bitcast_fusion
  13.0 0.8 copy.62
  13.8 1.6 gather_fusion.1
  15.4 0.6 convolution_convert_fusion.3
  16.0 0.8 convolution_convert_fusion.1
  16.8 2.5 copy.35
  19.3 17.4 %all-to-all-start = ((bf16[128,32,256]{2,1,0:T(8,128)(2,1)}), bf16[128,32,256]{2,1,0:T(8,128)(2,1)}, u32[]{:S(2)}, u32[]{:S(2)}) async-start(bf16[128,32,256]{2,1,0:T(8,128)(2,1)} %copy.35), calls=%async_computation | async-start | bytes 4194304 | tf_op jit(solution)/shard_map/all_to_all | solution.py:85
  36.7 0.6 convert_element_type.45
  37.4 0.8 pad_maximum_fusion.11
  38.3 2.4 collective-permute-start
  40.7 3.1 collective-permute-start.1
  43.9 147.5 %all-gather.4.cloned.1.call-done = bf16[32,16384]{1,0:T(8,128)(2,1)} async-done(((bf16[32,256]{1,0:T(8,128)(2,1)}), bf16[32,16384]{1,0:T(8,128)(2,1)}) %all-gather.4.cloned.1.call-update) | async-done | bytes 1048592 | tf_op jit(solution)/shard_map/all_gather | solution.py:64
  191.4 2.3 copy.60
  193.7 2.7 gather_fusion
  196.4 3.1 fusion.18
  199.5 1.0 broadcast.73.clone
  200.5 6.8 scatter_fusion
  207.3 3.2 fusion.24
  210.5 0.8 copy.61
  211.4 1.6 gather_fusion.3
  213.0 0.6 convolution_convert_fusion.2
  213.5 0.8 convolution_convert_fusion
  214.4 2.5 copy.40
  216.9 8.6 all-to-all-start.1
  225.5 2.0 convert_reduce_fusion.1
  227.5 93.5 %all-to-all-done.1 = bf16[128,32,256]{2,1,0:T(8,128)(2,1)} async-done(((bf16[128,32,256]{2,1,0:T(8,128)(2,1)}), bf16[128,32,256]{2,1,0:T(8,128)(2,1)}, u32[]{:S(2)}, u32[]{:S(2)}) %all-to-all-start.1) | async-done | bytes 2097184 | tf_op jit(solution)/shard_map/all_to_all | solution.py:85
  321.0 2.0 convert_reduce_fusion
  322.9 0.6 fusion.51
  323.7 1.3 multiply_bitcast_fusion.2
  325.0 0.9 copy-done.1
  326.1 3.1 collective-permute-start.2
  329.1 3.2 collective-permute-start.3
  332.3 101.7 %all-gather.6.cloned.1.call-done = bf16[32,16384]{1,0:T(8,128)(2,1)} async-done(((bf16[32,256]{1,0:T(8,128)(2,1)}), bf16[32,16384]{1,0:T(8,128)(2,1)}) %all-gather.6.cloned.1.call-update) | async-done | bytes 1048592 | tf_op jit(solution)/shard_map/all_gather | solution.py:64
  434.0 2.4 copy.59
  436.4 2.7 gather_fusion.2
  439.1 3.1 fusion.16
  442.2 1.0 broadcast.73
  443.2 6.8 scatter_fusion.1
  450.0 3.6 fusion.49
  453.6 62.9 %all_gather.15 = bf16[256,256]{1,0:T(8,128)(2,1)S(1)} all-gather(bf16[32,256]{1,0:T(8,128)(2,1)S(1)} %get-tuple-element.7), channel_id=1, replica_groups=mesh['seg'=64,'vec'=8] {'vec'}, dimensions={0}, use_global_device_ids=true | all-gather | bytes 147456 | tf_op jit(solution)/shard_map/all_gather | solution.py:106
  516.7 84.7 %all-gather.8.cloned.1.call-done = bf16[256,6144]{1,0:T(8,128)(2,1)} async-done(((bf16[32,6144]{1,0:T(8,128)(2,1)}), bf16[256,6144]{1,0:T(8,128)(2,1)}) %all-gather.8.cloned.1.call-update) | async-done | bytes 3145744 | tf_op jit(solution)/shard_map/all_gather | solution.py:100
  601.4 3.1 convolution_add_fusion
  604.5 409.7 %psum.7 = f32[32,256]{1,0:T(8,128)S(1)} all-reduce(f32[32,256]{1,0:T(8,128)S(1)} %convolution_add_fusion), channel_id=1, replica_groups=mesh['seg'=64,'vec'=8] {'seg'}, use_global_device_ids=true, to_apply=%region_8.11 | all-reduce | flops 8192 | bytes 65536 | tf_op jit(solution)/shard_map/psum | solution.py:110
  1014.1 0.6 broadcast_multiply_fusion
  (38 shorter events, 0.9 us)
Async XLA Ops:
  7.2 8.2 copy-start
  19.3 17.4 %copy-start.4 = (f32[32,256]{1,0:T(8,128)S(1)}, f32[32,256]{1,0:T(8,128)}, u32[]{:S(2)}) copy-start(f32[32,256]{1,0:T(8,128)} %param.13) | copy-start | bytes 98308
  19.3 24.6 %copy-start.7 = (s32[44,1]{0,1:T(1,128)S(1)}, s32[44,1]{0,1:T(1,128)}, u32[]{:S(2)}) copy-start(s32[44,1]{0,1:T(1,128)} %param.18) | copy-start | bytes 532
  19.3 197.6 %all-to-all-start = ((bf16[128,32,256]{2,1,0:T(8,128)(2,1)}), bf16[128,32,256]{2,1,0:T(8,128)(2,1)}, u32[]{:S(2)}, u32[]{:S(2)}) async-start(bf16[128,32,256]{2,1,0:T(8,128)(2,1)} %copy.35), calls=%async_computation | async-start | bytes 4194304 | tf_op jit(solution)/shard_map/all_to_all | solution.py:85
  36.7 154.7 %all-gather.4.cloned.1.call-start = ((), (), s32[]{:S(2)}) async-start(), calls=%async_computation.2 | async-start | bytes 1064960 | tf_op jit(solution)/shard_map/all_gather | solution.py:64
  38.3 169.0 %collective-permute-start = (f32[2,32,1]{2,1,0:T(8,128)S(1)}, f32[2,32,1]{2,1,0:T(8,128)S(1)}, u32[]{:S(2)}, u32[]{:S(2)}) collective-permute-start(f32[2,32,1]{2,1,0:T(8,128)S(1)} %get-tuple-element.15), channel_id=1, source_target_pairs={{8,0},{16,8},{24,16},{32,24},{40,32},{48,40},{56,48},{64,56},{72,6... | collective-permute-start | bytes 776 | tf_op jit(solution)/shard_map/ppermute | solution.py:22
  40.7 166.6 %collective-permute-start.1 = (f32[2,32,1]{2,1,0:T(8,128)S(1)}, f32[2,32,1]{2,1,0:T(8,128)S(1)}, u32[]{:S(2)}, u32[]{:S(2)}) collective-permute-start(f32[2,32,1]{2,1,0:T(8,128)S(1)} %get-tuple-element.16), channel_id=1, source_target_pairs={{0,8},{8,16},{16,24},{24,32},{32,40},{40,48},{48,56},{56,64},{64,7... | collective-permute-start | bytes 776 | tf_op jit(solution)/shard_map/ppermute | solution.py:21
  196.4 10.9 %copy-start.3 = (f32[6144]{0:T(1024)S(1)}, f32[6144]{0:T(1024)}, u32[]{:S(2)}) copy-start(f32[6144]{0:T(1024)} %param.15) | copy-start | bytes 73732
  196.4 10.9 %copy-start.5 = (f32[6144]{0:T(1024)S(1)}, f32[6144]{0:T(1024)}, u32[]{:S(2)}) copy-start(f32[6144]{0:T(1024)} %param.14) | copy-start | bytes 73732
  216.9 8.6 copy-start.6
  216.9 104.1 %all-to-all-start.1 = ((bf16[128,32,256]{2,1,0:T(8,128)(2,1)}), bf16[128,32,256]{2,1,0:T(8,128)(2,1)}, u32[]{:S(2)}, u32[]{:S(2)}) async-start(bf16[128,32,256]{2,1,0:T(8,128)(2,1)} %copy.40), calls=%async_computation.1 | async-start | bytes 4194304 | tf_op jit(solution)/shard_map/all_to_all | solution.py:85
  225.5 208.5 %all-gather.6.cloned.1.call-start = ((), (), s32[]{:S(2)}) async-start(), calls=%async_computation.3 | async-start | bytes 1064960 | tf_op jit(solution)/shard_map/all_gather | solution.py:64
  323.6 277.8 %all-gather.8.cloned.1.call-start = ((), (), s32[]{:S(2)}) async-start(), calls=%async_computation.4 | async-start | bytes 3538944 | tf_op jit(solution)/shard_map/all_gather | solution.py:100
  324.9 0.9 copy-start.1
  324.9 1.1 copy-start.2
  326.1 123.9 %collective-permute-start.2 = (f32[2,32,1]{2,1,0:T(8,128)S(1)}, f32[2,32,1]{2,1,0:T(8,128)S(1)}, u32[]{:S(2)}, u32[]{:S(2)}) collective-permute-start(f32[2,32,1]{2,1,0:T(8,128)S(1)} %get-tuple-element.13), channel_id=1, source_target_pairs={{8,0},{16,8},{24,16},{32,24},{40,32},{48,40},{56,48},{64,56},{72,6... | collective-permute-start | bytes 776 | tf_op jit(solution)/shard_map/ppermute | solution.py:22
  329.1 120.9 %collective-permute-start.3 = (f32[2,32,1]{2,1,0:T(8,128)S(1)}, f32[2,32,1]{2,1,0:T(8,128)S(1)}, u32[]{:S(2)}, u32[]{:S(2)}) collective-permute-start(f32[2,32,1]{2,1,0:T(8,128)S(1)} %get-tuple-element.14), channel_id=1, source_target_pairs={{0,8},{8,16},{16,24},{24,32},{32,40},{40,48},{48,56},{56,64},{64,7... | collective-permute-start | bytes 776 | tf_op jit(solution)/shard_map/ppermute | solution.py:21
Sparse Core Ops, SparseCore 0:
  40.2 151.1 all-gather.3
  323.7 110.2 all-gather.5
  453.7 147.6 all-gather.7
where the time goes:
time: 1030 us; the launch traced here: 1020 us
  blocking collectives  473 us (46%)
  waiting for transfers between devices  427 us (41%)
  starting transfers between devices  37.9 us (4%)
  other arithmetic  34.2 us (3%)
  local copies, waits for them, and re-layouts  23.1 us (2%)
  between operations  14 us (1%)
  matrix products  12.2 us (1%)
    psum x1, blocking collectives, body(): summed_gram = lax.psum(products, 'seg')  410 us
    all_gather x2, waiting for transfers between devices, operate(): lax.all_gather(mode_part.astype(jnp.bfloat16), 'seg', axis=1, tiled=True)  249 us
    all_to_all x2, waiting for transfers between devices, operate(): lax.all_to_all(buffered, 'seg', split_axis=0, concat_axis=0, tiled=True)  93.5 us
    all_gather x1, waiting for transfers between devices, body(): lax.all_gather(rounded_line, 'vec', axis=0, tiled=True)  84.7 us
    all_gather x1, blocking collectives, body(): lax.all_gather(rounded_mode, 'vec', axis=0, tiled=True)  62.9 us
    all_to_all x2, starting transfers between devices, operate(): lax.all_to_all(buffered, 'seg', split_axis=0, concat_axis=0, tiled=True)  25.9 us
  transfers between devices with their start and end apart: 9, of which 4 were waited for; matrix products, arithmetic and copies ran while one was open for 5% of the time, Pallas kernels for 0%

commit v1 on v0

v1 whole, which is shorter than its diff:
```python
import jax
import jax.numpy as jnp
from jax import lax
from jax.experimental import pallas as pl
from jax.experimental.pallas import tpu as pltpu
from jax.sharding import PartitionSpec as P

F32 = jnp.float32
BF16 = jnp.bfloat16
I32 = jnp.int32
PANEL = 128
PANELS = 24
SLOTS = 48
ATT = 44
COLS = 32
MB = 256
TOTAL = 393216 + 16384
MESH = pl.DeviceIdType.MESH
NT = (((1,), (1,)), ((), ()))

AG = (0, 16)
RS = (32, 48)
HALO = (64, 66)
GRAM = 72
MODE = 80
PLANE = 88
ZSUM = 120
LAST = 136
MESSAGES = 144


def tables_kernel(att, counts, tab):
    c0 = counts[0, 0]

    def clear(i, _):
        tab[i] = 0
        tab[64 + i] = 64
        tab[128 + i] = SLOTS
        tab[192 + i] = SLOTS
        return 0

    lax.fori_loop(0, 64, clear, 0, unroll=8)

    def one(t, _):
        slot = jnp.where(t < c0, t, t - c0 + PANELS)
        o = att[t, 0]
        z = o // 8
        pos = (z % 2) * 4 + (z // 2 % 2) * 2 + z // 4
        block = (o % 2) * 32 + (o // 2 % 4) * 8 + pos
        tab[slot] = t
        tab[64 + slot] = block
        first = tab[128 + block]
        free = first == SLOTS
        tab[192 + block] = jnp.where(free, SLOTS, slot)
        tab[128 + block] = jnp.where(free, slot, first)
        return 0

    lax.fori_loop(0, ATT, one, 0, unroll=4)


def kernel(
    tab, x_ref, y_ref, diag, links, stiff, tiles,
    line_out, mode_out, gram_out,
    g1, g2, out, s_buf, c_buf, r_buf, z_buf, xe, we, halo, w_mode, fb, gb, fm, mb, g_acc, p_buf, p_recv, q_buf, q_recv, last,
    send, recv,
):
    s = lax.axis_index("seg")
    v = lax.axis_index("vec")
    core, x, z = s % 2, s // 2 % 4, s // 8
    yy, zh = v // 2, v % 2
    pos = (z % 2) * 4 + (z // 2 % 2) * 2 + z // 4
    xr, xl, xo = (x + 1) % 4, (x + 3) % 4, (x + 2) % 4
    pc = 1 - core
    started = []

    def seg_of(zz, xx, cc):
        return zz * 8 + xx * 2 + cc

    def flip(a, n):
        return a + n - 2 * n * (a // n % 2)

    partner = seg_of(z, x, pc)
    right, left = seg_of(z, xr, core), seg_of(z, xl, core)
    z_peer = (seg_of(flip(z, 4), x, core), seg_of(flip(z, 2), x, core), seg_of(flip(z, 1), x, core))

    def copy(i, src, dst, seg, vec=None):
        return pltpu.make_async_remote_copy(
            src_ref=src, dst_ref=dst, send_sem=send.at[i], recv_sem=recv.at[i],
            device_id=(seg, v if vec is None else vec), device_id_type=MESH,
        )

    def go(i, src, dst, seg, vec=None):
        c = copy(i, src, dst, seg, vec)
        c.start()
        started.append(c)

    def got(i, dst):
        copy(i, dst, dst, partner).wait_recv()

    lane = lax.broadcasted_iota(I32, (COLS, PANEL), 1)

    def ag_start(r, g, mode):
        g[64] = jnp.zeros((COLS, MB), BF16)
        mine = core * 32 + x * 8 + pos
        g[mine] = mode.astype(BF16)
        go(AG[r], g.at[pl.ds(mine, 1)], g.at[pl.ds(mine, 1)], z_peer[0])

    def ag_z(r, g, step):
        have = (1, 2)[step]
        row = core * 32 + x * 8
        theirs = row + flip(pos // have * have, have)
        got(AG[r] + step, g.at[pl.ds(theirs, have)])
        run = row + pos // (2 * have) * (2 * have)
        go(AG[r] + step + 1, g.at[pl.ds(run, 2 * have)], g.at[pl.ds(run, 2 * have)], z_peer[step + 1])

    def ag_x(r, g):
        row = core * 32 + x * 8
        got(AG[r] + 2, g.at[pl.ds(row + 4 - pos // 4 * 4, 4)])
        mine = g.at[pl.ds(row, 8)]
        go(AG[r] + 3, mine, mine, right)
        go(AG[r] + 4, mine, mine, left)
        go(AG[r] + 7, mine, mine, partner)

    def ag_forward(r, g):
        from_left = g.at[pl.ds(core * 32 + xl * 8, 8)]
        got(AG[r] + 3, from_left)
        half = g.at[pl.ds(core * 32 + xl * 8, 4)]
        go(AG[r] + 5, half, half, right)
        go(AG[r] + 8, from_left, from_left, partner)
        from_right = g.at[pl.ds(core * 32 + xr * 8, 8)]
        got(AG[r] + 4, from_right)
        half = g.at[pl.ds(core * 32 + xr * 8 + 4, 4)]
        go(AG[r] + 6, half, half, left)
        go(AG[r] + 9, from_right, from_right, partner)

    def ag_opposite(r, g):
        for part in (0, 1):
            far = g.at[pl.ds(core * 32 + xo * 8 + part * 4, 4)]
            got(AG[r] + 5 + part, far)
            go(AG[r] + 10 + part, far, far, partner)

    def ag_end(r, g):
        for i, xx in ((7, x), (8, xl), (9, xr)):
            got(AG[r] + i, g.at[pl.ds(pc * 32 + xx * 8, 8)])
        for part in (0, 1):
            got(AG[r] + 10 + part, g.at[pl.ds(pc * 32 + xo * 8 + part * 4, 4)])

    def outgoing(src, low, high):
        def one(q, _):
            panel = src[q].astype(BF16)
            out[q] = jnp.dot(panel, tiles[tab[q]], preferred_element_type=F32).astype(BF16)
            return 0

        lax.fori_loop(low, high, one, 0, unroll=4)

    def sums(r, base):
        def one(i, _):
            b = base + i
            s_buf[r, b] = out[tab[128 + b]].astype(F32) + out[tab[192 + b]].astype(F32)
            return 0

        lax.fori_loop(0, 8, one, 0, unroll=4)

    def rs_core(r):
        for i, xx in enumerate((xo, xr, xl, x)):
            sums(r, pc * 32 + xx * 8)
            go(RS[r] + i, s_buf.at[r, pl.ds(pc * 32 + xx * 8, 8)], c_buf.at[r, pl.ds(xx * 8, 8)], partner)
        for xx in (xo, xr, xl, x):
            sums(r, core * 32 + xx * 8)

    def add(r, base, ref, start, n):
        def one(i, _):
            s_buf[r, base + i] = s_buf[r, base + i] + ref[r, start + i]
            return 0

        lax.fori_loop(0, n, one, 0, unroll=min(n, 4))

    def rs_x_first(r):
        for i, xx in enumerate((xo, xr, xl, x)):
            got(RS[r] + i, c_buf.at[r, pl.ds(xx * 8, 8)])
            base = core * 32 + xx * 8
            add(r, base, c_buf, xx * 8, 8)
            if i == 0:
                go(RS[r] + 4, s_buf.at[r, pl.ds(base, 4)], r_buf.at[r, pl.ds(0, 4)], right)
                go(RS[r] + 5, s_buf.at[r, pl.ds(base + 4, 4)], r_buf.at[r, pl.ds(4, 4)], left)
            if i == 1:
                go(RS[r] + 6, s_buf.at[r, pl.ds(base + 4, 4)], r_buf.at[r, pl.ds(12, 4)], right)
            if i == 2:
                go(RS[r] + 7, s_buf.at[r, pl.ds(base, 4)], r_buf.at[r, pl.ds(16, 4)], left)

    def rs_x_second(r):
        got(RS[r] + 4, r_buf.at[r, pl.ds(0, 4)])
        base = core * 32 + xr * 8
        add(r, base, r_buf, 0, 4)
        go(RS[r] + 8, s_buf.at[r, pl.ds(base, 4)], r_buf.at[r, pl.ds(8, 4)], right)
        got(RS[r] + 5, r_buf.at[r, pl.ds(4, 4)])
        base = core * 32 + xl * 8 + 4
        add(r, base, r_buf, 4, 4)
        go(RS[r] + 9, s_buf.at[r, pl.ds(base, 4)], r_buf.at[r, pl.ds(20, 4)], left)

    def rs_x_end(r):
        base = core * 32 + x * 8
        for i, at, half in ((6, 12, 4), (7, 16, 0), (8, 8, 0), (9, 20, 4)):
            got(RS[r] + i, r_buf.at[r, pl.ds(at, 4)])
            add(r, base + half, r_buf, at, 4)

    def rs_z_send(r, step):
        n, at = ((4, 0), (2, 4), (1, 6))[step]
        run = core * 32 + x * 8 + flip(pos // n * n, n)
        go(RS[r] + 10 + step, s_buf.at[r, pl.ds(run, n)], z_buf.at[r, pl.ds(at, n)], z_peer[2 - step])

    def rs_z_add(r, step):
        n, at = ((4, 0), (2, 4), (1, 6))[step]
        got(RS[r] + 10 + step, z_buf.at[r, pl.ds(at, n)])
        add(r, core * 32 + x * 8 + pos // n * n, z_buf, at, n)

    def halo_send(r, src):
        halo[r, 2] = src[SLOTS - 1] * links[pl.ds(SLOTS - 1, 1), :]
        go(HALO[r], src.at[0], halo.at[r, 0], (s + 63) % 64)
        go(HALO[r] + 1, halo.at[r, 2], halo.at[r, 1], (s + 1) % 64)

    def halo_take(r, src):
        got(HALO[r], halo.at[r, 0])
        got(HALO[r] + 1, halo.at[r, 1])
        src[SLOTS] = jnp.where(s < 63, halo[r, 0], 0.0)
        halo[r, 3] = jnp.where(s > 0, halo[r, 1], 0.0)

    def shifted(r, src, g, q, before):
        here = src[q]
        link = links[pl.ds(q, 1), :]
        linked = link * here
        after = jnp.where(lane == PANEL - 1, pltpu.roll(src[q + 1], PANEL - 1, 1), pltpu.roll(here, PANEL - 1, 1))
        prior = jnp.where(lane == 0, pltpu.roll(before, 1, 1), pltpu.roll(linked, 1, 1))
        coupled = lax.dot_general(g[tab[64 + q]], tiles[tab[q]], NT, preferred_element_type=F32)
        return (diag[pl.ds(q, 1), :] - 3.0) * here - link * after - prior + coupled, linked

    def stiffened(mode):
        wide = jnp.concatenate([stiff[pl.ds(0, 1), :], stiff[pl.ds(1, 1), :]], 1) - 3.0
        return wide * mode

    for q in range(SLOTS):
        xe[q] = x_ref[:, q * PANEL : (q + 1) * PANEL]
    out[SLOTS] = jnp.zeros((COLS, MB), BF16)
    ag_start(0, g1, y_ref[...])
    halo_send(0, xe)
    outgoing(xe, 0, 16)
    ag_z(0, g1, 0)
    outgoing(xe, 16, 32)
    ag_z(0, g1, 1)
    outgoing(xe, 32, 48)
    rs_core(0)
    ag_x(0, g1)
    rs_x_first(0)
    ag_forward(0, g1)
    rs_x_second(0)
    ag_opposite(0, g1)
    halo_take(0, xe)
    ag_end(0, g1)

    def first_panel(q, before):
        image, linked = shifted(0, xe, g1, q, before)
        we[q] = image * 0.4
        return linked

    lax.fori_loop(0, SLOTS, first_panel, halo[0, 3], unroll=4)
    halo_send(1, we)
    rs_x_end(0)
    rs_z_send(0, 0)
    outgoing(we, 0, 24)
    rs_z_add(0, 0)
    rs_z_send(0, 1)
    outgoing(we, 24, 48)
    rs_z_add(0, 1)
    rs_z_send(0, 2)
    rs_core(1)
    rs_z_add(0, 2)
    w_mode[...] = (stiffened(y_ref[...]) + s_buf[0, core * 32 + x * 8 + pos]) * 0.4

    ag_start(1, g2, w_mode[...])
    rs_x_first(1)
    ag_z(1, g2, 0)
    ag_z(1, g2, 1)
    ag_x(1, g2)
    rs_x_second(1)
    ag_forward(1, g2)
    halo_take(1, we)
    ag_opposite(1, g2)
    rs_x_end(1)
    rs_z_send(1, 0)
    ag_end(1, g2)

    def second_panel(q, before):
        image, linked = shifted(1, we, g2, q, before)
        value = image * 0.8 - xe[q]
        line_out[:, pl.ds(pl.multiple_of(q * PANEL, PANEL), PANEL)] = value
        fb[q] = value.astype(BF16)
        return linked

    far_first = ((0, 1), (1, 1), (2, 1), (3, 1), (1, 0), (2, 0), (3, 0), (0, 0))
    for dy, dz in far_first:
        k = (yy + dy) % 4 * 2 + (zh + dz) % 2
        q0 = k * 6
        ahead = jnp.maximum(q0 - 1, 0)
        before = jnp.where(q0 > 0, links[pl.ds(ahead, 1), :] * we[ahead], halo[1, 3])
        lax.fori_loop(0, 6, lambda i, b, q0=q0: second_panel(q0 + i, b), before, unroll=3)
        if (dy, dz) != (0, 0):
            go(GRAM + dy * 2 + dz, fb.at[pl.ds(q0, 6)], gb.at[v], s, k)

    rs_z_add(1, 0)
    rs_z_send(1, 1)
    gb[v] = fb[pl.ds(v * 6, 6)]
    rs_z_add(1, 1)
    rs_z_send(1, 2)
    rs_z_add(1, 2)
    filtered = (stiffened(w_mode[...]) + s_buf[1, core * 32 + x * 8 + pos]) * 0.8 - y_ref[...]
    mode_out[...] = filtered
    fm[...] = filtered.astype(BF16)

    keeper = s % 8

    def mode_number(one, other):
        return MODE + (one // 2 - other // 2 + 4) % 4 * 2 + (one + other) % 2

    @pl.when(v != keeper)
    def _():
        copy(mode_number(keeper, v), fm, mb.at[v], s, keeper).start()

    @pl.when(v == keeper)
    def _():
        mb[v] = fm[...]

    for dy, dz in far_first[4:7] + far_first[:4]:
        frm = (yy + 4 - dy) % 4 * 2 + (zh + dz) % 2
        got(GRAM + dy * 2 + dz, gb.at[frm])
    wide = jnp.concatenate([gb[:, p].reshape(8 * COLS, PANEL) for p in range(6)], 1)
    g_acc[...] = lax.dot_general(wide, wide, NT, preferred_element_type=F32)

    @pl.when(v != keeper)
    def _():
        copy(mode_number(keeper, v), fm, mb.at[v], s, keeper).wait_send()

    @pl.when(v == keeper)
    def _():
        for dy, dz in far_first[:7]:
            frm = (yy + 4 - dy) % 4 * 2 + (zh + dz) % 2
            got(MODE + dy * 2 + dz, mb.at[frm])
        modes = mb[...].reshape(8 * COLS, MB)
        g_acc[...] += lax.dot_general(modes, modes, NT, preferred_element_type=F32)

    for y1 in range(4):
        for x1 in range(4):
            for c1 in range(2):
                for h1 in range(2):
                    row = (y1 * 2 + h1) * 32 + x1 * 8
                    p_buf[(y1 * 4 + x1) * 2 + c1, h1] = g_acc[row : row + 8, c1 * 128 : c1 * 128 + 128]

    def plane_copy(r):
        w1 = (yy + r // 8) % 4, (x + r // 2 % 4) % 4, (core + r % 2) % 2
        src = p_buf.at[(w1[0] * 4 + w1[1]) * 2 + w1[2]]
        return copy(PLANE + r, src, p_recv.at[r], seg_of(z, w1[1], w1[2]), w1[0] * 2 + zh)

    def start_plane(r, _):
        plane_copy(r).start()
        return 0

    lax.fori_loop(1, 32, start_plane, 0)

    def take_plane(r, total):
        got(PLANE + r, p_recv.at[r])
        return total + p_recv[r]

    mine = (yy * 4 + x) * 2 + core
    q_buf[...] = lax.fori_loop(1, 32, take_plane, p_buf[mine])

    def z_copy(r):
        u = (zh * 8 + z + r) % 16
        return copy(ZSUM + r, q_buf.at[u // 8], q_recv.at[r], seg_of(u % 8, x, core), yy * 2 + u // 8)

    def start_z(r, _):
        z_copy(r).start()
        return 0

    lax.fori_loop(1, 16, start_z, 0)

    def take_z(r, total):
        got(ZSUM + r, q_recv.at[r])
        return total + q_recv[r]

    j = x * 2 + core
    last[j] = lax.fori_loop(1, 16, take_z, q_buf[zh]) * (1.0 / TOTAL)

    def last_copy(r):
        j1 = (j + r) % 8
        return copy(LAST + r, last.at[j], last.at[j], seg_of(z, j1 // 2, j1 % 2))

    for r in range(1, 8):
        last_copy(r).start()
    for r in range(1, 8):
        got(LAST + r, last.at[(j + 8 - r) % 8])
    for j1 in range(8):
        gram_out[j1 // 2 * 8 : j1 // 2 * 8 + 8, j1 % 2 * 128 : j1 % 2 * 128 + 128] = last[j1]

    for c in started:
        c.wait_send()

    def end_plane(r, _):
        plane_copy(r).wait_send()
        return 0

    lax.fori_loop(1, 32, end_plane, 0)

    def end_z(r, _):
        z_copy(r).wait_send()
        return 0

    lax.fori_loop(1, 16, end_z, 0)
    for r in range(1, 8):
        last_copy(r).wait_send()


def body(line_vectors, mode_vectors, line_diagonal, line_links, stiffness, coupling_tiles, attachments, block_counts):
    tab = pl.pallas_call(
        tables_kernel,
        out_shape=jax.ShapeDtypeStruct((256,), I32),
        in_specs=[pl.BlockSpec(memory_space=pltpu.SMEM)] * 2,
        out_specs=pl.BlockSpec(memory_space=pltpu.SMEM),
    )(attachments, block_counts)
    block = (COLS, MB)
    return pl.pallas_call(
        kernel,
        out_shape=(
            jax.ShapeDtypeStruct((COLS, SLOTS * PANEL), F32),
            jax.ShapeDtypeStruct(block, F32),
            jax.ShapeDtypeStruct((COLS, 8 * COLS), F32),
        ),
        in_specs=[pl.BlockSpec(memory_space=pltpu.SMEM)] + [pl.BlockSpec(memory_space=pltpu.VMEM)] * 6,
        out_specs=[pl.BlockSpec(memory_space=pltpu.VMEM)] * 3,
        scratch_shapes=[
            pltpu.VMEM((65,) + block, BF16),
            pltpu.VMEM((65,) + block, BF16),
            pltpu.VMEM((SLOTS + 1,) + block, BF16),
            pltpu.VMEM((2, 64) + block, F32),
            pltpu.VMEM((2, 32) + block, F32),
            pltpu.VMEM((2, 24) + block, F32),
            pltpu.VMEM((2, 7) + block, F32),
            pltpu.VMEM((SLOTS + 1, COLS, PANEL), F32),
            pltpu.VMEM((SLOTS + 1, COLS, PANEL), F32),
            pltpu.VMEM((2, 4, COLS, PANEL), F32),
            pltpu.VMEM(block, F32),
            pltpu.VMEM((SLOTS, COLS, PANEL), BF16),
            pltpu.VMEM((8, 6, COLS, PANEL), BF16),
            pltpu.VMEM(block, BF16),
            pltpu.VMEM((8,) + block, BF16),
            pltpu.VMEM((256, 256), F32),
            pltpu.VMEM((32, 2, 8, 128), F32),
            pltpu.VMEM((32, 2, 8, 128), F32),
            pltpu.VMEM((2, 8, 128), F32),
            pltpu.VMEM((16, 8, 128), F32),
            pltpu.VMEM((8, 8, 128), F32),
            pltpu.SemaphoreType.DMA((MESSAGES,)),
            pltpu.SemaphoreType.DMA((MESSAGES,)),
        ],
        compiler_params=pltpu.CompilerParams(has_side_effects=True, vmem_limit_bytes=50 * 2**20),
    )(
        tab,
        line_vectors,
        mode_vectors,
        line_diagonal.reshape(SLOTS, PANEL),
        line_links.reshape(SLOTS, PANEL),
        stiffness.reshape(2, PANEL),
        coupling_tiles,
    )


def solution(mesh):
    in_specs = (
        P("vec", "seg"),
        P("vec", "seg"),
        P("seg"),
        P("seg"),
        P("seg"),
        P("seg", None, None),
        P("seg", None),
        P("seg", None),
    )
    out_specs = (P("vec", "seg"), P("vec", "seg"), P("vec", None))
    return jax.shard_map(body, mesh=mesh, in_specs=in_specs, out_specs=out_specs, check_vma=False)
```

time: 1030 us -> 158 us (0.15)
  blocking collectives: 473 us -> 0 us
  waiting for transfers between devices: 427 us -> 0 us
  Pallas kernels: 0 us -> 148 us
  starting transfers between devices: 37.9 us -> 0 us
  other arithmetic: 34.2 us -> 0 us
  local copies, waits for them, and re-layouts: 23.1 us -> 8.18 us
  between operations: 14 us -> 0.66 us
  matrix products: 12.2 us -> 0 us
    psum x1 -> x0, blocking collectives: 410 us -> none  [body(): summed_gram = lax.psum(products, 'seg')]
    all_gather x3 -> x0, waiting for transfers between devices: 334 us -> none  [the longest x2 249 us: operate(): lax.all_gather(mode_part.astype(jnp.bfloat16), 'seg', axis=1, tiled=True)]
    pallas_call x0 -> x2, Pallas kernels: none -> 148 us  [the longest x1 145 us: body(): pl.pallas_call(kernel, out_shape=(jax.ShapeDtypeStruct((COLS, SLOTS * PAN...]
    all_to_all x2 -> x0, waiting for transfers between devices: 93.5 us -> none  [operate(): lax.all_to_all(buffered, 'seg', split_axis=0, concat_axis=0, tiled=True)]
    all_gather x1 -> x0, blocking collectives: 62.9 us -> none  [body(): lax.all_gather(rounded_mode, 'vec', axis=0, tiled=True)]
    all_to_all x2 -> x0, starting transfers between devices: 25.9 us -> none  [operate(): lax.all_to_all(buffered, 'seg', split_axis=0, concat_axis=0, tiled=True)]
    scatter-add x2 -> x0, other arithmetic: 13.6 us -> none  [operate(): coupled = jnp.zeros((columns, line_rows // PANEL, PANEL), jnp.float32).at...]
    dot_general x8 -> x0, matrix products: 12.2 us -> none  [the longest x2 6.18 us: operate(): jnp.einsum('vtm,tpm->vtp', picked, coupling_tiles, preferred_element_type...]
  transfers between devices with their start and end apart: 9 -> 0, of which waited for: 4 -> 0; matrix products, arithmetic and copies ran while one was open for 5% -> 0% of each run, Pallas kernels for 0% -> 0%
where the time goes in v1:
time: 158 us; the launch traced here: 157 us
  Pallas kernels  148 us (94%)
  local copies, waits for them, and re-layouts  8.18 us (5%)
    pallas_call x1, Pallas kernels, body(): pl.pallas_call(kernel, out_shape=(jax.ShapeDtypeStruct((COLS, SLOTS * PAN...  145 us
    unnamed x16, local copies, waits for them, and re-layouts  8.18 us

profile of v1, /device:TPU:1, one launch (start us, length us, event | category | flops | bytes accessed | tf_op | source)
XLA Modules:
  0.0 157.0 jit_solution(1378311744244386949)
XLA Ops:
  0.6 1.4 copy.11.att
  2.0 3.1 %shard_map.103.tab = s32[256]{0:T(256)} custom-call(s32[44,1]{1,0:T(8,128)} %copy.11.att, s32[1,2]{1,0:T(1,128)} %counts.1), custom_call_target="tpu_custom_call" | custom-call | tf_op jit(solution)/shard_map/pallas_call | solution.py:422
  5.1 0.0 copy-start
  5.1 1.1 copy-done
  6.2 0.0 copy-start.1
  6.3 0.8 copy-done.1
  7.0 0.0 copy-start.2
  7.0 0.7 copy-done.2
  7.7 0.0 copy-start.3
  7.7 0.7 copy-done.3
  8.5 0.0 copy-start.4
  8.5 0.7 copy-done.4
  9.2 0.0 copy-start.5
  9.2 0.7 copy-done.5
  9.8 145.1 %shard_map.104 = (f32[32,6144]{1,0:T(8,128)S(1)}, f32[32,256]{1,0:T(8,128)S(1)}, f32[32,256]{1,0:T(8,128)S(1)}) custom-call(s32[256]{0:T(256)S(1)} %copy-done.4, f32[32,6144]{1,0:T(8,128)S(1)} %copy-done, f32[32,256]{1,0:T(8,128)S(1)} %copy-done.1, f32[48,128]{1,0:T(8,128)S(1)} %bitcast.3, f32[48,128]{1,0:T(8,128)S(1)} %bitcast.4, f32[2,128]{1,0:T(2,128)S(1)} %bitcast.5, ...), custom_call_target="tpu_custom_call" | custom-call | tf_op jit(solution)/shard_map/pallas_call | solution.py:429
  154.9 0.9 copy.15
  155.8 0.6 copy.16
  156.4 0.6 copy.17
Async XLA Ops:
  5.1 1.1 copy-start
  6.2 0.8 copy-start.1
  7.0 0.7 copy-start.2
  7.7 0.7 copy-start.3
  8.5 0.7 copy-start.4
  9.2 0.7 copy-start.5

commit v2 on v1

v2 whole, which is shorter than its diff:
```python
import jax
import jax.numpy as jnp
from jax import lax
from jax.experimental import pallas as pl
from jax.experimental.pallas import tpu as pltpu
from jax.sharding import PartitionSpec as P

F32 = jnp.float32
BF16 = jnp.bfloat16
I32 = jnp.int32
PANEL = 128
PANELS = 24
SLOTS = 48
ATT = 44
COLS = 32
MB = 256
TOTAL = 393216 + 16384
MESH = pl.DeviceIdType.MESH
NT = (((1,), (1,)), ((), ()))

AG = (0, 24)
RS = (48, 88)
HALO = (128, 130)
GRAM = 136
MODE = 144
PLANE = 152
ZSUM = 184
LAST = 200
MESSAGES = 208
FAR = (4, 5, 6, 7, 2, 3, 1, 0)


def kernel(
    att, counts, x_hbm, y_hbm, diag_hbm, links_hbm, stiff_hbm, tiles_hbm, att_hbm,
    line_out, mode_out, gram_out,
    x_ref, y_ref, diag, links, stiff, tiles, owner_row, tab_v, tab,
    g1, g2, out, s_buf, c_buf, r_buf, z_buf, xe, we, halo, w_mode, fb, gb, fm, mb, g_acc, p_buf, p_recv, q_buf, q_recv, last,
    send, recv, load,
):
    s = lax.axis_index("seg")
    v = lax.axis_index("vec")
    core, x, z = s % 2, s // 2 % 4, s // 8
    yy, zh = v // 2, v % 2
    pc = 1 - core
    started = []

    def seg_of(zz, xx, cc):
        return zz * 8 + xx * 2 + cc

    def flip(a, n):
        for bit in (1, 2, 4):
            if n & bit:
                a = a + bit - 2 * bit * (a // bit % 2)
        return a

    partner = seg_of(z, x, pc)
    x_of = [(x + d) % 4 for d in range(4)]
    z_of = [flip(z, k) for k in range(8)]
    far_first = ((0, 1), (1, 1), (2, 1), (3, 1), (1, 0), (2, 0), (3, 0), (0, 0))

    barrier = pltpu.get_barrier_semaphore()
    peers = [(partner, v), ((s + 1) % 64, v), ((s + 63) % 64, v)]
    peers += [(seg_of(z, x_of[d], core), v) for d in (1, 2, 3)]
    peers += [(seg_of(z_of[k], x, core), v) for k in range(1, 8)]
    peers += [(s, (yy + dy) % 4 * 2 + (zh + dz) % 2) for dy, dz in far_first[:7]]
    for peer in peers:
        pl.semaphore_signal(barrier, inc=1, device_id=peer, device_id_type=MESH)

    pairs = [(x_hbm, x_ref), (y_hbm, y_ref), (diag_hbm, diag), (links_hbm, links), (stiff_hbm, stiff), (att_hbm, owner_row)]
    pairs += [(tiles_hbm.at[pl.ds(i * 11, 11)], tiles.at[pl.ds(i * 11, 11)]) for i in range(4)]
    loads = [pltpu.make_async_copy(a, b, load.at[i]) for i, (a, b) in enumerate(pairs)]
    for i in (5, 0, 6, 7, 8, 9, 1, 2, 3, 4):
        loads[i].start()

    def copy(i, src, dst, seg, vec=None):
        return pltpu.make_async_remote_copy(
            src_ref=src, dst_ref=dst, send_sem=send.at[i], recv_sem=recv.at[i],
            device_id=(seg, v if vec is None else vec), device_id_type=MESH,
        )

    def go(i, src, dst, seg, vec=None):
        c = copy(i, src, dst, seg, vec)
        c.start()
        started.append(c)

    def got(i, dst):
        copy(i, dst, dst, partner).wait_recv()

    lane = lax.broadcasted_iota(I32, (COLS, PANEL), 1)
    c0 = counts[0, 0]

    def block_of(owner):
        return owner % 2 * 32 + owner // 2 % 4 * 8 + owner // 8

    runs = ((z // 2 * 2, 2), (flip(z, 2) // 2 * 2, 2), (flip(z, 4) // 4 * 4, 4))

    def ag_start(r, g, mode):
        g[64] = jnp.zeros((COLS, MB), BF16)
        mine = core * 32 + x * 8 + z
        g[mine] = mode.astype(BF16)
        for k in (7, 6, 5, 4, 3, 2, 1):
            go(AG[r] + k, g.at[mine], g.at[mine], seg_of(z_of[k], x, core))

    def ag_x(r, g, piece):
        for k in ((1,), (2, 3), (4, 5, 6, 7))[piece]:
            got(AG[r] + k, g.at[core * 32 + x * 8 + z_of[k]])
        run = g.at[pl.ds(core * 32 + x * 8 + runs[piece][0], runs[piece][1])]
        for d in (2, 1, 3):
            go(AG[r] + 8 + piece * 3 + d - 1, run, run, seg_of(z, x_of[d], core))

    def ag_core(r, g):
        for d in (0, 1, 3, 2):
            row = core * 32 + x_of[-d % 4] * 8
            for piece in range(3) if d else ():
                got(AG[r] + 8 + piece * 3 + d - 1, g.at[pl.ds(row + runs[piece][0], runs[piece][1])])
            whole = g.at[pl.ds(row, 8)]
            go(AG[r] + 17 + d, whole, whole, partner)

    def ag_end(r, g):
        for d in (0, 1, 3, 2):
            got(AG[r] + 17 + d, g.at[pl.ds(pc * 32 + x_of[-d % 4] * 8, 8)])

    def outgoing(src, low, high):
        def one(t, _):
            slot = jnp.minimum(jnp.where(t < c0, t, t - c0 + PANELS), SLOTS - 1)
            out[t] = jnp.dot(src[slot].astype(BF16), tiles[t], preferred_element_type=F32).astype(BF16)
            return 0

        lax.fori_loop(low, high, one, 0, unroll=4 if high - low == 44 else high - low)

    def sums(r, cc, k):
        def one(xx, _):
            b = cc * 32 + xx * 8 + z_of[k]
            s_buf[r, cc, xx, z_of[k]] = out[tab[0, b, 0]].astype(F32) + out[tab[1, b, 0]].astype(F32)
            return 0

        lax.fori_loop(0, 4, one, 0, unroll=True)

    def rs_core(r, k):
        go(RS[r] + k, s_buf.at[r, pc, :, z_of[k]], c_buf.at[r, :, z_of[k]], partner)

    def rs_x(r, k):
        zk = z_of[k]
        got(RS[r] + k, c_buf.at[r, :, zk])
        for xx in range(4):
            s_buf[r, core, xx, zk] = s_buf[r, core, xx, zk] + c_buf[r, xx, zk]
        for d in (2, 1, 3):
            go(RS[r] + 8 + k * 3 + d - 1, s_buf.at[r, core, x_of[d], zk], r_buf.at[r, d - 1, k], seg_of(z, x_of[d], core))

    def rs_z(r, k):
        zk = z_of[k]
        for d in (1, 2, 3):
            got(RS[r] + 8 + k * 3 + d - 1, r_buf.at[r, d - 1, k])
        s_buf[r, core, x, zk] = s_buf[r, core, x, zk] + r_buf[r, 0, k] + r_buf[r, 1, k] + r_buf[r, 2, k]
        if k:
            go(RS[r] + 32 + k, s_buf.at[r, core, x, zk], z_buf.at[r, k], seg_of(zk, x, core))

    def rs_end(r):
        total = s_buf[r, core, x, z]
        for k in range(1, 8):
            got(RS[r] + 32 + k, z_buf.at[r, k])
            total = total + z_buf[r, k]
        return total

    def halo_send(r, src):
        halo[r, 2] = src[SLOTS - 1] * links[pl.ds(SLOTS - 1, 1), :]
        go(HALO[r], src.at[0], halo.at[r, 0], (s + 63) % 64)
        go(HALO[r] + 1, halo.at[r, 2], halo.at[r, 1], (s + 1) % 64)

    def halo_take(r, src):
        got(HALO[r], halo.at[r, 0])
        got(HALO[r] + 1, halo.at[r, 1])
        src[SLOTS] = jnp.where(s < 63, halo[r, 0], 0.0)
        halo[r, 3] = jnp.where(s > 0, halo[r, 1], 0.0)

    def shifted(r, src, g, q, before):
        here = src[q]
        link = links[pl.ds(q, 1), :]
        linked = link * here
        after = jnp.where(lane == PANEL - 1, pltpu.roll(src[q + 1], PANEL - 1, 1), pltpu.roll(here, PANEL - 1, 1))
        prior = jnp.where(lane == 0, pltpu.roll(before, 1, 1), pltpu.roll(linked, 1, 1))
        second = q >= PANELS
        rank = jnp.where(second, q - PANELS, q)
        t = jnp.minimum(jnp.where(second, rank + c0, rank), ATT - 1)
        used = rank < jnp.where(second, counts[0, 1], c0)
        block = jnp.where(used, block_of(att[0, t]), 64)
        coupled = lax.dot_general(g[block], tiles[t], NT, preferred_element_type=F32)
        return (diag[pl.ds(q, 1), :] - 3.0) * here - link * after - prior + coupled, linked

    def stiffened(mode):
        wide = jnp.concatenate([stiff[pl.ds(0, 1), :], stiff[pl.ds(1, 1), :]], 1) - 3.0
        return wide * mode

    loads[5].wait()
    owner = owner_row[...]
    at = lax.broadcasted_iota(I32, (64, ATT), 1)
    same = jnp.broadcast_to(block_of(owner), (64, ATT)) == lax.broadcasted_iota(I32, (64, ATT), 0)
    one = jnp.min(jnp.where(same, at, ATT), 1, keepdims=True)
    two = jnp.max(jnp.where(same, at, -1), 1, keepdims=True)
    tab_v[0] = jnp.broadcast_to(one, (64, 128))
    tab_v[1] = jnp.broadcast_to(jnp.where(two > one, two, ATT), (64, 128))
    to_scalars = pltpu.make_async_copy(tab_v, tab, load.at[10])
    to_scalars.start()
    out[ATT] = jnp.zeros((COLS, MB), BF16)
    loads[0].wait()
    for q in range(SLOTS):
        xe[q] = x_ref[:, q * PANEL : (q + 1) * PANEL]
    for i in range(4):
        loads[6 + i].wait()
        outgoing(xe, i * 11, i * 11 + 11)
    to_scalars.wait()
    for i in range(1, 5):
        loads[i].wait()
    for k in FAR:
        sums(0, pc, k)
        sums(0, core, k)
    pl.semaphore_wait(barrier, len(peers))
    for k in FAR[:2]:
        rs_core(0, k)
    ag_start(0, g1, y_ref[...])
    for k in FAR[2:]:
        rs_core(0, k)
    for k in FAR:
        rs_x(0, k)
    halo_send(0, xe)
    for k in FAR[:2]:
        rs_z(0, k)
    ag_x(0, g1, 0)
    ag_x(0, g1, 1)
    for k in FAR[2:4]:
        rs_z(0, k)
    ag_x(0, g1, 2)
    for k in FAR[4:]:
        rs_z(0, k)
    ag_core(0, g1)
    halo_take(0, xe)
    ag_end(0, g1)

    def first_panel(q, before):
        image, linked = shifted(0, xe, g1, q, before)
        we[q] = image * 0.4
        return linked

    lax.fori_loop(0, SLOTS, first_panel, halo[0, 3], unroll=4)
    halo_send(1, we)
    w_mode[...] = (stiffened(y_ref[...]) + rs_end(0)) * 0.4

    ag_start(1, g2, w_mode[...])
    outgoing(we, 0, 44)
    for k in FAR:
        sums(1, pc, k)
        rs_core(1, k)
    for k in FAR:
        sums(1, core, k)
    for k in FAR[:2]:
        rs_x(1, k)
    for piece in range(3):
        ag_x(1, g2, piece)
    for k in FAR[2:]:
        rs_x(1, k)
    for k in FAR[:2]:
        rs_z(1, k)
    halo_take(1, we)
    ag_core(1, g2)
    for k in FAR[2:4]:
        rs_z(1, k)
    ag_end(1, g2)

    def second_panel(q, before):
        image, linked = shifted(1, we, g2, q, before)
        value = image * 0.8 - xe[q]
        line_out[:, pl.ds(pl.multiple_of(q * PANEL, PANEL), PANEL)] = value
        fb[q] = value.astype(BF16)
        return linked

    for dy, dz in far_first:
        k = (yy + dy) % 4 * 2 + (zh + dz) % 2
        q0 = k * 6
        ahead = jnp.maximum(q0 - 1, 0)
        before = jnp.where(q0 > 0, links[pl.ds(ahead, 1), :] * we[ahead], halo[1, 3])
        lax.fori_loop(0, 6, lambda i, b, q0=q0: second_panel(q0 + i, b), before, unroll=3)
        if (dy, dz) != (0, 0):
            go(GRAM + dy * 2 + dz, fb.at[pl.ds(q0, 6)], gb.at[v], s, k)

    gb[v] = fb[pl.ds(v * 6, 6)]
    for k in FAR[4:]:
        rs_z(1, k)
    filtered = (stiffened(w_mode[...]) + rs_end(1)) * 0.8 - y_ref[...]
    mode_out[...] = filtered
    fm[...] = filtered.astype(BF16)

    keeper = s % 8

    def mode_number(one, other):
        return MODE + (one // 2 - other // 2 + 4) % 4 * 2 + (one + other) % 2

    @pl.when(v != keeper)
    def _():
        copy(mode_number(keeper, v), fm, mb.at[v], s, keeper).start()

    @pl.when(v == keeper)
    def _():
        mb[v] = fm[...]

    for dy, dz in far_first[4:7] + far_first[:4]:
        frm = (yy + 4 - dy) % 4 * 2 + (zh + dz) % 2
        got(GRAM + dy * 2 + dz, gb.at[frm])
    wide = jnp.concatenate([gb[:, p].reshape(8 * COLS, PANEL) for p in range(6)], 1)
    g_acc[...] = lax.dot_general(wide, wide, NT, preferred_element_type=F32)

    @pl.when(v != keeper)
    def _():
        copy(mode_number(keeper, v), fm, mb.at[v], s, keeper).wait_send()

    @pl.when(v == keeper)
    def _():
        for dy, dz in far_first[:7]:
            frm = (yy + 4 - dy) % 4 * 2 + (zh + dz) % 2
            got(MODE + dy * 2 + dz, mb.at[frm])
        modes = mb[...].reshape(8 * COLS, MB)
        g_acc[...] += lax.dot_general(modes, modes, NT, preferred_element_type=F32)

    for y1 in range(4):
        for x1 in range(4):
            for c1 in range(2):
                for h1 in range(2):
                    row = (y1 * 2 + h1) * 32 + x1 * 8
                    p_buf[(y1 * 4 + x1) * 2 + c1, h1] = g_acc[row : row + 8, c1 * 128 : c1 * 128 + 128]

    def plane_copy(r):
        w1 = (yy + r // 8) % 4, (x + r // 2 % 4) % 4, (core + r % 2) % 2
        src = p_buf.at[(w1[0] * 4 + w1[1]) * 2 + w1[2]]
        return copy(PLANE + r, src, p_recv.at[r], seg_of(z, w1[1], w1[2]), w1[0] * 2 + zh)

    def start_plane(r, _):
        plane_copy(r).start()
        return 0

    lax.fori_loop(1, 32, start_plane, 0)

    def take_plane(r, total):
        got(PLANE + r, p_recv.at[r])
        return total + p_recv[r]

    mine = (yy * 4 + x) * 2 + core
    q_buf[...] = lax.fori_loop(1, 32, take_plane, p_buf[mine])

    def z_copy(r):
        u = (zh * 8 + z + r) % 16
        return copy(ZSUM + r, q_buf.at[u // 8], q_recv.at[r], seg_of(u % 8, x, core), yy * 2 + u // 8)

    def start_z(r, _):
        z_copy(r).start()
        return 0

    lax.fori_loop(1, 16, start_z, 0)

    def take_z(r, total):
        got(ZSUM + r, q_recv.at[r])
        return total + q_recv[r]

    j = x * 2 + core
    last[j] = lax.fori_loop(1, 16, take_z, q_buf[zh]) * (1.0 / TOTAL)

    def last_copy(r):
        j1 = (j + r) % 8
        return copy(LAST + r, last.at[j], last.at[j], seg_of(z, j1 // 2, j1 % 2))

    for r in range(1, 8):
        last_copy(r).start()
    for r in range(1, 8):
        got(LAST + r, last.at[(j + 8 - r) % 8])
    for j1 in range(8):
        gram_out[j1 // 2 * 8 : j1 // 2 * 8 + 8, j1 % 2 * 128 : j1 % 2 * 128 + 128] = last[j1]

    for c in started:
        c.wait_send()

    def end_plane(r, _):
        plane_copy(r).wait_send()
        return 0

    lax.fori_loop(1, 32, end_plane, 0)

    def end_z(r, _):
        z_copy(r).wait_send()
        return 0

    lax.fori_loop(1, 16, end_z, 0)
    for r in range(1, 8):
        last_copy(r).wait_send()


def body(line_vectors, mode_vectors, line_diagonal, line_links, stiffness, coupling_tiles, attachments, block_counts):
    block = (COLS, MB)
    owners = attachments.reshape(1, ATT)
    return pl.pallas_call(
        kernel,
        out_shape=(
            jax.ShapeDtypeStruct((COLS, SLOTS * PANEL), F32),
            jax.ShapeDtypeStruct(block, F32),
            jax.ShapeDtypeStruct((COLS, 8 * COLS), F32),
        ),
        in_specs=[pl.BlockSpec(memory_space=pltpu.SMEM)] * 2 + [pl.BlockSpec(memory_space=pltpu.HBM)] * 7,
        out_specs=[pl.BlockSpec(memory_space=pltpu.VMEM)] * 3,
        scratch_shapes=[
            pltpu.VMEM((COLS, SLOTS * PANEL), F32),
            pltpu.VMEM(block, F32),
            pltpu.VMEM((SLOTS, PANEL), F32),
            pltpu.VMEM((SLOTS, PANEL), F32),
            pltpu.VMEM((2, PANEL), F32),
            pltpu.VMEM((ATT, PANEL, MB), BF16),
            pltpu.VMEM((1, ATT), I32),
            pltpu.VMEM((2, 64, 128), I32),
            pltpu.SMEM((2, 64, 128), I32),
            pltpu.VMEM((65,) + block, BF16),
            pltpu.VMEM((65,) + block, BF16),
            pltpu.VMEM((ATT + 1,) + block, BF16),
            pltpu.VMEM((2, 2, 4, 8) + block, F32),
            pltpu.VMEM((2, 4, 8) + block, F32),
            pltpu.VMEM((2, 3, 8) + block, F32),
            pltpu.VMEM((2, 8) + block, F32),
            pltpu.VMEM((SLOTS + 1, COLS, PANEL), F32),
            pltpu.VMEM((SLOTS + 1, COLS, PANEL), F32),
            pltpu.VMEM((2, 4, COLS, PANEL), F32),
            pltpu.VMEM(block, F32),
            pltpu.VMEM((SLOTS, COLS, PANEL), BF16),
            pltpu.VMEM((8, 6, COLS, PANEL), BF16),
            pltpu.VMEM(block, BF16),
            pltpu.VMEM((8,) + block, BF16),
            pltpu.VMEM((256, 256), F32),
            pltpu.VMEM((32, 2, 8, 128), F32),
            pltpu.VMEM((32, 2, 8, 128), F32),
            pltpu.VMEM((2, 8, 128), F32),
            pltpu.VMEM((16, 8, 128), F32),
            pltpu.VMEM((8, 8, 128), F32),
            pltpu.SemaphoreType.DMA((MESSAGES,)),
            pltpu.SemaphoreType.DMA((MESSAGES,)),
            pltpu.SemaphoreType.DMA((11,)),
        ],
        compiler_params=pltpu.CompilerParams(
            has_side_effects=True, collective_id=0, vmem_limit_bytes=64 * 2**20
        ),
    )(
        owners,
        block_counts,
        line_vectors,
        mode_vectors,
        line_diagonal.reshape(SLOTS, PANEL),
        line_links.reshape(SLOTS, PANEL),
        stiffness.reshape(2, PANEL),
        coupling_tiles,
        owners,
    )


def solution(mesh):
    in_specs = (
        P("vec", "seg"),
        P("vec", "seg"),
        P("seg"),
        P("seg"),
        P("seg"),
        P("seg", None, None),
        P("seg", None),
        P("seg", None),
    )
    out_specs = (P("vec", "seg"), P("vec", "seg"), P("vec", None))
    return jax.shard_map(body, mesh=mesh, in_specs=in_specs, out_specs=out_specs, check_vma=False)
```

time: 158 us -> 120 us (0.76)
  Pallas kernels: 148 us -> 115 us
  local copies, waits for them, and re-layouts: 8.18 us -> 4.81 us
    pallas_call x1, Pallas kernels: 145 us -> 115 us  [body(): pl.pallas_call(kernel, out_shape=(jax.ShapeDtypeStruct((COLS, SLOTS * PAN...]
    unnamed x16 -> x3, local copies, waits for them, and re-layouts: 8.18 us -> 4.81 us
    pallas_call x1 -> x0, Pallas kernels: 3.12 us -> none  [body(): pl.pallas_call(tables_kernel, out_shape=jax.ShapeDtypeStruct((256,), I32)...]
where the time goes in v2:
time: 120 us
  Pallas kernels  115 us (96%)
  local copies, waits for them, and re-layouts  4.81 us (4%)
    pallas_call x1, Pallas kernels, body(): pl.pallas_call(kernel, out_shape=(jax.ShapeDtypeStruct((COLS, SLOTS * PAN...  115 us
    unnamed x3, local copies, waits for them, and re-layouts  4.81 us

profile of v2, /device:TPU:1, one launch (start us, length us, event | category | flops | bytes accessed | tf_op | source)
XLA Modules:
  0.0 120.0 jit_solution(10290842203590654875)
XLA Ops:
  0.6 114.5 %shard_map.103 = (f32[32,6144]{1,0:T(8,128)}, f32[32,256]{1,0:T(8,128)}, f32[32,256]{1,0:T(8,128)}) custom-call(s32[1,44]{1,0:T(1,128)} %bitcast.6, s32[1,2]{1,0:T(1,128)} %counts.1, f32[32,6144]{1,0:T(8,128)} %x_hbm.1, f32[32,256]{1,0:T(8,128)} %y_hbm.1, f32[48,128]{1,0:T(8,128)} %bitcast.4, f32[48,128]{1,0:T(8,128)} %bitcast.5, f32[2,128]{1,0:T(2,128)} %bitcast.8, ...), custom_call_target="tpu_custom_call" | custom-call | tf_op jit(solution)/shard_map/pallas_call | solution.py:397
  115.1 2.1 %copy.14 = f32[32,6144]{1,0:T(8,128)} copy(f32[32,6144]{1,0:T(8,128)} %get-tuple-element.6) | data formatting | bytes 1572864
  117.2 1.4 %copy.15 = f32[32,256]{1,0:T(8,128)} copy(f32[32,256]{1,0:T(8,128)} %get-tuple-element.7) | data formatting | bytes 65536
  118.6 1.4 %copy.16 = f32[32,256]{1,0:T(8,128)} copy(f32[32,256]{1,0:T(8,128)} %get-tuple-element.8) | data formatting | bytes 65536

commit v3 on v2

--- a/solution.py
+++ b/solution.py
@@ -19,15 +19,15 @@
 NT = (((1,), (1,)), ((), ()))
 
 AG = (0, 24)
-RS = (48, 88)
-HALO = (128, 130)
-GRAM = 136
-MODE = 144
-PLANE = 152
-ZSUM = 184
-LAST = 200
-MESSAGES = 208
-FAR = (4, 5, 6, 7, 2, 3, 1, 0)
+RS = (48, 96)
+HALO = (144, 146)
+GRAM = 152
+MODE = 160
+PLANE = 168
+ZSUM = 200
+LAST = 216
+MESSAGES = 224
+ORDER = (7, 6, 5, 4, 3, 2, 1, 0)
 
 
 def kernel(
@@ -139,26 +139,47 @@
     def rs_core(r, k):
         go(RS[r] + k, s_buf.at[r, pc, :, z_of[k]], c_buf.at[r, :, z_of[k]], partner)
 
-    def rs_x(r, k):
+    def add_core(r, k):
         zk = z_of[k]
         got(RS[r] + k, c_buf.at[r, :, zk])
         for xx in range(4):
             s_buf[r, core, xx, zk] = s_buf[r, core, xx, zk] + c_buf[r, xx, zk]
-        for d in (2, 1, 3):
-            go(RS[r] + 8 + k * 3 + d - 1, s_buf.at[r, core, x_of[d], zk], r_buf.at[r, d - 1, k], seg_of(z, x_of[d], core))
+
+    def rs_x1(r, k):
+        add_core(r, k)
+        via = 3 if k % 2 else 1
+        for n, to, d in ((0, 2, via), (1, 4 - via, 4 - via)):
+            src = s_buf.at[r, core, x_of[to], z_of[k]]
+            go(RS[r] + 10 + k * 3 + n, src, r_buf.at[r, n, k], seg_of(z, x_of[d], core))
+
+    def rs_x2(r, k):
+        to = x_of[3 if k % 2 else 1]
+        got(RS[r] + 10 + k * 3, r_buf.at[r, 0, k])
+        s_buf[r, core, to, z_of[k]] = s_buf[r, core, to, z_of[k]] + r_buf[r, 0, k]
+        go(RS[r] + 12 + k * 3, s_buf.at[r, core, to, z_of[k]], r_buf.at[r, 2, k], seg_of(z, to, core))
 
     def rs_z(r, k):
         zk = z_of[k]
-        for d in (1, 2, 3):
-            got(RS[r] + 8 + k * 3 + d - 1, r_buf.at[r, d - 1, k])
-        s_buf[r, core, x, zk] = s_buf[r, core, x, zk] + r_buf[r, 0, k] + r_buf[r, 1, k] + r_buf[r, 2, k]
-        if k:
-            go(RS[r] + 32 + k, s_buf.at[r, core, x, zk], z_buf.at[r, k], seg_of(zk, x, core))
+        total = s_buf[r, core, x, zk]
+        for n in (1, 2):
+            got(RS[r] + 10 + k * 3 + n, r_buf.at[r, n, k])
+            total = total + r_buf[r, n, k]
+        s_buf[r, core, x, zk] = total
+        if k % 4:
+            go(RS[r] + 34 + k, s_buf.at[r, core, x, zk], z_buf.at[r, k], seg_of(z_of[k % 4], x, core))
+
+    def rs_far(r):
+        total = s_buf[r, core, x, z_of[4]]
+        for k in (5, 6, 7):
+            got(RS[r] + 34 + k, z_buf.at[r, k])
+            total = total + z_buf[r, k]
+        s_buf[r, core, x, z_of[4]] = total
+        go(RS[r] + 38, s_buf.at[r, core, x, z_of[4]], z_buf.at[r, 4], seg_of(z_of[4], x, core))
 
     def rs_end(r):
         total = s_buf[r, core, x, z]
-        for k in range(1, 8):
-            got(RS[r] + 32 + k, z_buf.at[r, k])
+        for k in (1, 2, 3, 4):
+            got(RS[r] + 34 + k, z_buf.at[r, k])
             total = total + z_buf[r, k]
         return total
 
@@ -211,28 +232,33 @@
     to_scalars.wait()
     for i in range(1, 5):
         loads[i].wait()
-    for k in FAR:
+    for k in ORDER:
         sums(0, pc, k)
         sums(0, core, k)
     pl.semaphore_wait(barrier, len(peers))
-    for k in FAR[:2]:
+    for k in ORDER[:2]:
         rs_core(0, k)
     ag_start(0, g1, y_ref[...])
-    for k in FAR[2:]:
+    for k in ORDER[2:]:
         rs_core(0, k)
-    for k in FAR:
-        rs_x(0, k)
+    for k in (7, 6, 5, 4):
+        rs_x1(0, k)
     halo_send(0, xe)
-    for k in FAR[:2]:
-        rs_z(0, k)
     ag_x(0, g1, 0)
     ag_x(0, g1, 1)
-    for k in FAR[2:4]:
+    for k in (7, 6, 5, 4):
+        rs_x2(0, k)
+    for k in (3, 2, 1, 0):
+        rs_x1(0, k)
+    ag_x(0, g1, 2)
+    for k in (7, 6, 5, 4):
         rs_z(0, k)
-    ag_x(0, g1, 2)
-    for k in FAR[4:]:
+    for k in (3, 2, 1, 0):
+        rs_x2(0, k)
+    ag_core(0, g1)
+    rs_far(0)
+    for k in (3, 2, 1, 0):
         rs_z(0, k)
-    ag_core(0, g1)
     halo_take(0, xe)
     ag_end(0, g1)
 
@@ -243,27 +269,33 @@
 
     lax.fori_loop(0, SLOTS, first_panel, halo[0, 3], unroll=4)
     halo_send(1, we)
-    w_mode[...] = (stiffened(y_ref[...]) + rs_end(0)) * 0.4
-
-    ag_start(1, g2, w_mode[...])
+
     outgoing(we, 0, 44)
-    for k in FAR:
+    for k in ORDER:
         sums(1, pc, k)
         rs_core(1, k)
-    for k in FAR:
+    for k in ORDER:
         sums(1, core, k)
-    for k in FAR[:2]:
-        rs_x(1, k)
-    for piece in range(3):
-        ag_x(1, g2, piece)
-    for k in FAR[2:]:
-        rs_x(1, k)
-    for k in FAR[:2]:
+    w_mode[...] = (stiffened(y_ref[...]) + rs_end(0)) * 0.4
+    ag_start(1, g2, w_mode[...])
+    for k in ORDER[:6]:
+        rs_x1(1, k)
+    for k in (7, 6, 5, 4):
+        rs_x2(1, k)
+    ag_x(1, g2, 0)
+    ag_x(1, g2, 1)
+    rs_x1(1, 1)
+    rs_x1(1, 0)
+    ag_x(1, g2, 2)
+    for k in (7, 6, 5, 4):
+        rs_z(1, k)
+    for k in (3, 2, 1, 0):
+        rs_x2(1, k)
+    rs_far(1)
+    ag_core(1, g2)
+    for k in (3, 2, 1, 0):
         rs_z(1, k)
     halo_take(1, we)
-    ag_core(1, g2)
-    for k in FAR[2:4]:
-        rs_z(1, k)
     ag_end(1, g2)
 
     def second_panel(q, before):
@@ -273,27 +305,26 @@
         fb[q] = value.astype(BF16)
         return linked
 
-    for dy, dz in far_first:
+    def row_chunk(dy, dz):
         k = (yy + dy) % 4 * 2 + (zh + dz) % 2
         q0 = k * 6
         ahead = jnp.maximum(q0 - 1, 0)
         before = jnp.where(q0 > 0, links[pl.ds(ahead, 1), :] * we[ahead], halo[1, 3])
-        lax.fori_loop(0, 6, lambda i, b, q0=q0: second_panel(q0 + i, b), before, unroll=3)
+        lax.fori_loop(0, 6, lambda i, b: second_panel(q0 + i, b), before, unroll=3)
         if (dy, dz) != (0, 0):
             go(GRAM + dy * 2 + dz, fb.at[pl.ds(q0, 6)], gb.at[v], s, k)
 
-    gb[v] = fb[pl.ds(v * 6, 6)]
-    for k in FAR[4:]:
-        rs_z(1, k)
+    keeper = s % 8
+
+    def mode_number(one, other):
+        return MODE + (one // 2 - other // 2 + 4) % 4 * 2 + (one + other) % 2
+
+    for dy, dz in far_first[:4]:
+        row_chunk(dy, dz)
     filtered = (stiffened(w_mode[...]) + rs_end(1)) * 0.8 - y_ref[...]
     mode_out[...] = filtered
     fm[...] = filtered.astype(BF16)
 
-    keeper = s % 8
-
-    def mode_number(one, other):
-        return MODE + (one // 2 - other // 2 + 4) % 4 * 2 + (one + other) % 2
-
     @pl.when(v != keeper)
     def _():
         copy(mode_number(keeper, v), fm, mb.at[v], s, keeper).start()
@@ -301,6 +332,10 @@
     @pl.when(v == keeper)
     def _():
         mb[v] = fm[...]
+
+    for dy, dz in far_first[4:]:
+        row_chunk(dy, dz)
+    gb[v] = fb[pl.ds(v * 6, 6)]
 
     for dy, dz in far_first[4:7] + far_first[:4]:
         frm = (yy + 4 - dy) % 4 * 2 + (zh + dz) % 2

time: 120 us -> 116 us (0.967)
  Pallas kernels: 115 us -> 110 us
    pallas_call x1, Pallas kernels: 115 us -> 110 us  [body(): pl.pallas_call(kernel, out_shape=(jax.ShapeDtypeStruct((COLS, SLOTS * PAN...]
where the time goes in v3:
time: 116 us
  Pallas kernels  110 us (95%)
  local copies, waits for them, and re-layouts  4.81 us (4%)
    pallas_call x1, Pallas kernels, body(): pl.pallas_call(kernel, out_shape=(jax.ShapeDtypeStruct((COLS, SLOTS * PAN...  110 us
    unnamed x3, local copies, waits for them, and re-layouts  4.81 us

profile of v3, /device:TPU:1, one launch (start us, length us, event | category | flops | bytes accessed | tf_op | source)
XLA Modules:
  0.0 115.7 jit_solution(5221973143730104271)
XLA Ops:
  0.6 110.3 %shard_map.103 = (f32[32,6144]{1,0:T(8,128)}, f32[32,256]{1,0:T(8,128)}, f32[32,256]{1,0:T(8,128)}) custom-call(s32[1,44]{1,0:T(1,128)} %bitcast.6, s32[1,2]{1,0:T(1,128)} %counts.1, f32[32,6144]{1,0:T(8,128)} %x_hbm.1, f32[32,256]{1,0:T(8,128)} %y_hbm.1, f32[48,128]{1,0:T(8,128)} %bitcast.4, f32[48,128]{1,0:T(8,128)} %bitcast.5, f32[2,128]{1,0:T(2,128)} %bitcast.8, ...), custom_call_target="tpu_custom_call" | custom-call | tf_op jit(solution)/shard_map/pallas_call | solution.py:432
  110.9 2.1 %copy.14 = f32[32,6144]{1,0:T(8,128)} copy(f32[32,6144]{1,0:T(8,128)} %get-tuple-element.6) | data formatting | bytes 1572864
  113.0 1.4 %copy.15 = f32[32,256]{1,0:T(8,128)} copy(f32[32,256]{1,0:T(8,128)} %get-tuple-element.7) | data formatting | bytes 65536
  114.4 1.4 %copy.16 = f32[32,256]{1,0:T(8,128)} copy(f32[32,256]{1,0:T(8,128)} %get-tuple-element.8) | data formatting | bytes 65536

commit v4 on v3

--- a/solution.py
+++ b/solution.py
@@ -34,7 +34,7 @@
     att, counts, x_hbm, y_hbm, diag_hbm, links_hbm, stiff_hbm, tiles_hbm, att_hbm,
     line_out, mode_out, gram_out,
     x_ref, y_ref, diag, links, stiff, tiles, owner_row, tab_v, tab,
-    g1, g2, out, s_buf, c_buf, r_buf, z_buf, xe, we, halo, w_mode, fb, gb, fm, mb, g_acc, p_buf, p_recv, q_buf, q_recv, last,
+    g1, g2, out, s_buf, c_buf, r_buf, z_buf, xe, we, halo, w_mode, fb, gb, fm, mb, g_acc, p_buf, p_core, p_recv, q_buf, q_recv, last,
     send, recv, load,
 ):
     s = lax.axis_index("seg")
@@ -92,7 +92,7 @@
     def block_of(owner):
         return owner % 2 * 32 + owner // 2 % 4 * 8 + owner // 8
 
-    runs = ((z // 2 * 2, 2), (flip(z, 2) // 2 * 2, 2), (flip(z, 4) // 4 * 4, 4))
+    runs = [flip(z, k) // 2 * 2 for k in (0, 2, 4, 6)]
 
     def ag_start(r, g, mode):
         g[64] = jnp.zeros((COLS, MB), BF16)
@@ -102,23 +102,23 @@
             go(AG[r] + k, g.at[mine], g.at[mine], seg_of(z_of[k], x, core))
 
     def ag_x(r, g, piece):
-        for k in ((1,), (2, 3), (4, 5, 6, 7))[piece]:
+        for k in ((1,), (2, 3), (4, 5), (6, 7))[piece]:
             got(AG[r] + k, g.at[core * 32 + x * 8 + z_of[k]])
-        run = g.at[pl.ds(core * 32 + x * 8 + runs[piece][0], runs[piece][1])]
+        run = g.at[pl.ds(core * 32 + x * 8 + runs[piece], 2)]
         for d in (2, 1, 3):
             go(AG[r] + 8 + piece * 3 + d - 1, run, run, seg_of(z, x_of[d], core))
 
     def ag_core(r, g):
         for d in (0, 1, 3, 2):
             row = core * 32 + x_of[-d % 4] * 8
-            for piece in range(3) if d else ():
-                got(AG[r] + 8 + piece * 3 + d - 1, g.at[pl.ds(row + runs[piece][0], runs[piece][1])])
+            for piece in range(4) if d else ():
+                got(AG[r] + 8 + piece * 3 + d - 1, g.at[pl.ds(row + runs[piece], 2)])
             whole = g.at[pl.ds(row, 8)]
-            go(AG[r] + 17 + d, whole, whole, partner)
+            go(AG[r] + 20 + d, whole, whole, partner)
 
     def ag_end(r, g):
         for d in (0, 1, 3, 2):
-            got(AG[r] + 17 + d, g.at[pl.ds(pc * 32 + x_of[-d % 4] * 8, 8)])
+            got(AG[r] + 20 + d, g.at[pl.ds(pc * 32 + x_of[-d % 4] * 8, 8)])
 
     def outgoing(src, low, high):
         def one(t, _):
@@ -126,7 +126,7 @@
             out[t] = jnp.dot(src[slot].astype(BF16), tiles[t], preferred_element_type=F32).astype(BF16)
             return 0
 
-        lax.fori_loop(low, high, one, 0, unroll=4 if high - low == 44 else high - low)
+        lax.fori_loop(low, high, one, 0, unroll=11)
 
     def sums(r, cc, k):
         def one(xx, _):
@@ -251,6 +251,7 @@
     for k in (3, 2, 1, 0):
         rs_x1(0, k)
     ag_x(0, g1, 2)
+    ag_x(0, g1, 3)
     for k in (7, 6, 5, 4):
         rs_z(0, k)
     for k in (3, 2, 1, 0):
@@ -267,7 +268,7 @@
         we[q] = image * 0.4
         return linked
 
-    lax.fori_loop(0, SLOTS, first_panel, halo[0, 3], unroll=4)
+    lax.fori_loop(0, SLOTS, first_panel, halo[0, 3], unroll=12)
     halo_send(1, we)
 
     outgoing(we, 0, 44)
@@ -287,6 +288,7 @@
     rs_x1(1, 1)
     rs_x1(1, 0)
     ag_x(1, g2, 2)
+    ag_x(1, g2, 3)
     for k in (7, 6, 5, 4):
         rs_z(1, k)
     for k in (3, 2, 1, 0):
@@ -310,7 +312,7 @@
         q0 = k * 6
         ahead = jnp.maximum(q0 - 1, 0)
         before = jnp.where(q0 > 0, links[pl.ds(ahead, 1), :] * we[ahead], halo[1, 3])
-        lax.fori_loop(0, 6, lambda i, b: second_panel(q0 + i, b), before, unroll=3)
+        lax.fori_loop(0, 6, lambda i, b: second_panel(q0 + i, b), before, unroll=True)
         if (dy, dz) != (0, 0):
             go(GRAM + dy * 2 + dz, fb.at[pl.ds(q0, 6)], gb.at[v], s, k)
 
@@ -360,25 +362,25 @@
             for c1 in range(2):
                 for h1 in range(2):
                     row = (y1 * 2 + h1) * 32 + x1 * 8
-                    p_buf[(y1 * 4 + x1) * 2 + c1, h1] = g_acc[row : row + 8, c1 * 128 : c1 * 128 + 128]
+                    p_buf[c1 * 16 + y1 * 4 + x1, h1] = g_acc[row : row + 8, c1 * 128 : c1 * 128 + 128]
+
+    go(PLANE, p_buf.at[pl.ds(pc * 16, 16)], p_core, partner)
+    got(PLANE, p_core)
+    for i in range(16):
+        p_buf[core * 16 + i] = p_buf[core * 16 + i] + p_core[i]
 
     def plane_copy(r):
-        w1 = (yy + r // 8) % 4, (x + r // 2 % 4) % 4, (core + r % 2) % 2
-        src = p_buf.at[(w1[0] * 4 + w1[1]) * 2 + w1[2]]
-        return copy(PLANE + r, src, p_recv.at[r], seg_of(z, w1[1], w1[2]), w1[0] * 2 + zh)
-
-    def start_plane(r, _):
+        y1, x1 = (yy + r // 4) % 4, (x + r % 4) % 4
+        src = p_buf.at[core * 16 + y1 * 4 + x1]
+        return copy(PLANE + r, src, p_recv.at[r], seg_of(z, x1, core), y1 * 2 + zh)
+
+    for r in (10, 9, 11, 6, 14, 5, 7, 13, 15, 2, 8, 1, 3, 4, 12):
         plane_copy(r).start()
-        return 0
-
-    lax.fori_loop(1, 32, start_plane, 0)
-
-    def take_plane(r, total):
+    total = p_buf[core * 16 + yy * 4 + x]
+    for r in range(1, 16):
         got(PLANE + r, p_recv.at[r])
-        return total + p_recv[r]
-
-    mine = (yy * 4 + x) * 2 + core
-    q_buf[...] = lax.fori_loop(1, 32, take_plane, p_buf[mine])
+        total = total + p_recv[r]
+    q_buf[...] = total
 
     def z_copy(r):
         u = (zh * 8 + z + r) % 16
@@ -388,14 +390,14 @@
         z_copy(r).start()
         return 0
 
-    lax.fori_loop(1, 16, start_z, 0)
+    lax.fori_loop(1, 16, start_z, 0, unroll=True)
 
     def take_z(r, total):
         got(ZSUM + r, q_recv.at[r])
         return total + q_recv[r]
 
     j = x * 2 + core
-    last[j] = lax.fori_loop(1, 16, take_z, q_buf[zh]) * (1.0 / TOTAL)
+    last[j] = lax.fori_loop(1, 16, take_z, q_buf[zh], unroll=True) * (1.0 / TOTAL)
 
     def last_copy(r):
         j1 = (j + r) % 8
@@ -411,17 +413,14 @@
     for c in started:
         c.wait_send()
 
-    def end_plane(r, _):
+    for r in range(1, 16):
         plane_copy(r).wait_send()
-        return 0
-
-    lax.fori_loop(1, 32, end_plane, 0)
 
     def end_z(r, _):
         z_copy(r).wait_send()
         return 0
 
-    lax.fori_loop(1, 16, end_z, 0)
+    lax.fori_loop(1, 16, end_z, 0, unroll=True)
     for r in range(1, 8):
         last_copy(r).wait_send()
 
@@ -465,7 +464,8 @@
             pltpu.VMEM((8,) + block, BF16),
             pltpu.VMEM((256, 256), F32),
             pltpu.VMEM((32, 2, 8, 128), F32),
-            pltpu.VMEM((32, 2, 8, 128), F32),
+            pltpu.VMEM((16, 2, 8, 128), F32),
+            pltpu.VMEM((16, 2, 8, 128), F32),
             pltpu.VMEM((2, 8, 128), F32),
             pltpu.VMEM((16, 8, 128), F32),
             pltpu.VMEM((8, 8, 128), F32),

time: 116 us -> 114 us (0.983)
  Pallas kernels: 110 us -> 108 us
    pallas_call x1, Pallas kernels: 110 us -> 108 us  [body(): pl.pallas_call(kernel, out_shape=(jax.ShapeDtypeStruct((COLS, SLOTS * PAN...]
where the time goes in v4:
time: 114 us
  Pallas kernels  108 us (95%)
  local copies, waits for them, and re-layouts  4.81 us (4%)
    pallas_call x1, Pallas kernels, body(): pl.pallas_call(kernel, out_shape=(jax.ShapeDtypeStruct((COLS, SLOTS * PAN...  108 us
    unnamed x3, local copies, waits for them, and re-layouts  4.81 us

profile of v4, /device:TPU:1, one launch (start us, length us, event | category | flops | bytes accessed | tf_op | source)
XLA Modules:
  0.0 113.6 jit_solution(15771212638263684308)
XLA Ops:
  0.6 108.2 %shard_map.103 = (f32[32,6144]{1,0:T(8,128)}, f32[32,256]{1,0:T(8,128)}, f32[32,256]{1,0:T(8,128)}) custom-call(s32[1,44]{1,0:T(1,128)} %bitcast.6, s32[1,2]{1,0:T(1,128)} %counts.1, f32[32,6144]{1,0:T(8,128)} %x_hbm.1, f32[32,256]{1,0:T(8,128)} %y_hbm.1, f32[48,128]{1,0:T(8,128)} %bitcast.4, f32[48,128]{1,0:T(8,128)} %bitcast.5, f32[2,128]{1,0:T(2,128)} %bitcast.8, ...), custom_call_target="tpu_custom_call" | custom-call | tf_op jit(solution)/shard_map/pallas_call | solution.py:431
  108.8 2.1 %copy.14 = f32[32,6144]{1,0:T(8,128)} copy(f32[32,6144]{1,0:T(8,128)} %get-tuple-element.6) | data formatting | bytes 1572864
  110.9 1.4 %copy.15 = f32[32,256]{1,0:T(8,128)} copy(f32[32,256]{1,0:T(8,128)} %get-tuple-element.7) | data formatting | bytes 65536
  112.3 1.4 %copy.16 = f32[32,256]{1,0:T(8,128)} copy(f32[32,256]{1,0:T(8,128)} %get-tuple-element.8) | data formatting | bytes 65536
